TPU v7x, 32 devices: a whole 2x2x4 slice. The times are simulated.
32 devices in a mesh: group: 2 (over y), patch: 4 (over z), head: 2 (over x), sub: 2 (over core).
Axes of the slice: x: 2, y: 2, z: 4, core: 2. Of those that a mesh axis runs over, the one named last changes fastest.
Arguments:
- qkv: bfloat16 [3, 16, 128, 3072], P(None, ('group', 'patch', 'sub'), 'head'), parts along dimension 1, may hold values from -64 to 64
- stale_kv: bfloat16 [2, 16, 128, 3072], P(None, ('group', 'patch', 'sub'), None, 'head'), parts along dimension 1, may hold values from -6 to 6
- w_out: bfloat16 [3072, 3072], P('head'), may hold values from -0.109375 to 0.109375
- neighbors: int32 [32, 6], P(('group', 'patch', 'sub')), parts along dimension 0, may hold values from 0 to 15, as said below
Outputs:
- block_output: bfloat16 [16, 128, 3072], P(('group', 'patch', 'sub'), 'head'), parts along dimension 0
There are 2 independent parts, one for each index of `group`. A program takes and returns all parts, laid end to end along the dimension named above; an argument that names none is the same for every part. Nothing has to cross between parts.
Inputs may be any that keep to these rules, and one draw needn't show every extreme that they name: `neighbors`: row g lists 6 distinct blocks; the first is g itself, the others lie within 3 block rows and one block column of g, where block g has block row g // 2 and block column g % 2.
All inputs are finite; a program needn't handle non-finite values.
Results may differ from a plain program's by a relative error of at most 0.0066.
Values may be sent and summed in bfloat16 or wider, within the bound.
A program may use at most 64 MiB of HBM per device.

v0:
```python
import math

import jax
import jax.numpy as jnp
from jax import lax
from jax.sharding import PartitionSpec as P

HD = 128
BLOCK = 64
NB = 6
REACH = 3


def passed_along(array, axis, by):
    peers = lax.axis_size(axis)
    pairs = [(i, i + by) for i in range(peers) if 0 <= i + by < peers]
    return lax.ppermute(array, axis, pairs)


def per_device(qkv, stale_kv, w_out, neighbors):
    columns = lax.all_to_all(qkv, "head", split_axis=3, concat_axis=2, tiled=True)
    tokens_here = columns.shape[2]
    width = columns.shape[3]
    local_heads = width // HD
    blocks = tokens_here // BLOCK
    pieces = {0: columns[1:3, 0]}
    for offset in range(-REACH, REACH + 1):
        if offset != 0:
            moved = passed_along(stale_kv, ("patch", "sub"), -offset)
            pieces[offset] = moved[:, 0]
    bank = jnp.stack([pieces[offset] for offset in range(-REACH, REACH + 1)], axis=0)
    bank = bank.reshape(2 * REACH + 1, 2, blocks, BLOCK, width)
    shard = lax.axis_index(("patch", "sub"))
    row_offset = neighbors // blocks - shard + REACH
    column = neighbors % blocks
    picked = bank[row_offset, :, column]
    keys = picked[:, :, 0].reshape(blocks, NB * BLOCK, local_heads, HD)
    values = picked[:, :, 1].reshape(blocks, NB * BLOCK, local_heads, HD)
    queries = columns[0, 0].reshape(blocks, BLOCK, local_heads, HD)
    scores = jnp.einsum(
        "bqhd,bkhd->bhqk", queries, keys, preferred_element_type=jnp.float32
    ) / math.sqrt(HD)
    top = jnp.max(scores, axis=-1, keepdims=True)
    expo = jnp.exp(scores - top)
    weights = (expo / jnp.sum(expo, axis=-1, keepdims=True)).astype(jnp.bfloat16)
    attended = jnp.einsum("bhqk,bkhd->bqhd", weights, values, preferred_element_type=jnp.float32)
    attended = attended.astype(jnp.bfloat16).reshape(tokens_here, width)
    rows_here = tokens_here // lax.axis_size("head")
    summed = lax.psum_scatter(
        jnp.dot(attended, w_out, preferred_element_type=jnp.float32).astype(jnp.bfloat16),
        "head",
        scatter_dimension=0,
        tiled=True,
    )
    return summed.reshape(1, rows_here, w_out.shape[1])


def solution(mesh):
    placed = (
        P(None, ("group", "patch", "sub"), "head", None),
        P(None, ("group", "patch", "sub"), None, "head"),
        P("head", None),
        P(("group", "patch", "sub"), None),
    )
    return jax.shard_map(
        per_device,
        mesh=mesh,
        in_specs=placed,
        out_specs=P(("group", "patch", "sub"), "head", None),
        check_vma=False,
    )
```

profile of v0, /device:TPU:1, one launch (start us, length us, event | category | flops | bytes accessed | tf_op | source)
XLA Modules:
  0.0 140.4 jit_solution(1060985702152121288)
XLA Ops:
  6.5 6.5 %collective-permute-start = (bf16[2,1,128,1536]{3,2,0,1:T(8,128)(2,1)}, bf16[2,1,128,1536]{3,2,0,1:T(8,128)(2,1)}, u32[]{:S(2)}, u32[]{:S(2)}) collective-permute-start(bf16[2,1,128,1536]{3,2,0,1:T(8,128)(2,1)} %bitcast.56), channel_id=1, source_target_pairs={{0,5},{1,8},{4,9},{5,12},{8,13},{2,7},{3,10},{6,11},{7,14},{10,15}... | collective-permute-start | bytes 2359304 | tf_op jit(solution)/shard_map/ppermute | solution.py:17
  13.0 4.6 %copy.46 = bf16[3,1,64,3072]{2,0,1,3:T(4,128)(2,1)S(1)} copy(bf16[3,1,64,3072]{3,2,1,0:T(8,128)(2,1)} %param.4) | data formatting | bytes 2359296 | tf_op args[0]
  17.6 0.0 copy-start.2
  17.6 3.0 %reshape.47 = bf16[2,2,147456]{2,1,0:T(2,128)(2,1)} reshape(bf16[3072,1,3,64]{3,2,1,0:T(4,128)(2,1)S(1)} %bitcast.51) | data formatting | bytes 2359296
  20.6 4.4 %all-to-all-start = ((bf16[2,2,147456]{2,1,0:T(2,128)(2,1)}), bf16[2,2,147456]{2,1,0:T(2,128)(2,1)}, u32[]{:S(2)}, u32[]{:S(2)}) async-start(bf16[2,2,147456]{2,1,0:T(2,128)(2,1)} %reshape.47), calls=%async_computation | async-start | bytes 2359296 | tf_op jit(solution)/shard_map/all_to_all | solution.py:21
  25.0 0.0 reduce-scatter.2.cloned.1.call-start
  25.1 3.2 %collective-permute-start.1 = (bf16[2,1,128,1536]{3,2,0,1:T(8,128)(2,1)}, bf16[2,1,128,1536]{3,2,0,1:T(8,128)(2,1)}, u32[]{:S(2)}, u32[]{:S(2)}) collective-permute-start(bf16[2,1,128,1536]{3,2,0,1:T(8,128)(2,1)} %bitcast.57), channel_id=1, source_target_pairs={{0,4},{1,5},{4,8},{5,9},{8,12},{9,13},{2,6},{3,7},{6,10},{7,11},{1... | collective-permute-start | bytes 2359304 | tf_op jit(solution)/shard_map/ppermute | solution.py:17
  28.3 1.9 %collective-permute-start.2 = (bf16[2,1,128,1536]{3,2,0,1:T(8,128)(2,1)}, bf16[2,1,128,1536]{3,2,0,1:T(8,128)(2,1)}, u32[]{:S(2)}, u32[]{:S(2)}) collective-permute-start(bf16[2,1,128,1536]{3,2,0,1:T(8,128)(2,1)} %bitcast.58), channel_id=1, source_target_pairs={{0,1},{1,4},{4,5},{5,8},{8,9},{9,12},{12,13},{2,3},{3,6},{6,7},{7,... | collective-permute-start | bytes 2359304 | tf_op jit(solution)/shard_map/ppermute | solution.py:17
  30.2 3.3 %collective-permute-start.3 = (bf16[2,1,128,1536]{3,2,0,1:T(8,128)(2,1)}, bf16[2,1,128,1536]{3,2,0,1:T(8,128)(2,1)}, u32[]{:S(2)}, u32[]{:S(2)}) collective-permute-start(bf16[2,1,128,1536]{3,2,0,1:T(8,128)(2,1)} %bitcast.59), channel_id=1, source_target_pairs={{1,0},{4,1},{5,4},{8,5},{9,8},{12,9},{13,12},{3,2},{6,3},{7,6},{10... | collective-permute-start | bytes 2359304 | tf_op jit(solution)/shard_map/ppermute | solution.py:17
  33.6 1.3 collective-permute-start.4
  34.9 0.0 copy-done.2
  34.9 0.1 reshape.29
  35.0 4.7 %all-to-all-done = bf16[2,2,147456]{2,1,0:T(2,128)(2,1)} async-done(((bf16[2,2,147456]{2,1,0:T(2,128)(2,1)}), bf16[2,2,147456]{2,1,0:T(2,128)(2,1)}, u32[]{:S(2)}, u32[]{:S(2)}) %all-to-all-start) | async-done | bytes 1179680 | tf_op jit(solution)/shard_map/all_to_all | solution.py:21
  39.7 3.0 %reshape.48 = bf16[3072,1,3,64]{3,2,1,0:T(4,128)(2,1)S(1)} reshape(bf16[2,2,147456]{2,1,0:T(2,128)(2,1)} %all-to-all-done) | data formatting | bytes 2359296
  42.7 3.2 %copy.48 = bf16[3,1,64,2,1536]{4,2,3,0,1:T(8,128)(2,1)} copy(bf16[3,1,64,2,1536]{2,0,4,3,1:T(4,128)(2,1)S(1)} %bitcast.50) | data formatting | bytes 2359296 | tf_op jit(solution)/shard_map/all_to_all | solution.py:21
  45.9 0.0 copy-start.1
  45.9 1.1 slice.22
  47.1 1.1 reshape_squeeze.11
  48.1 0.0 collective-permute-done
  48.1 1.3 collective-permute-start.5
  49.4 2.1 %constant_dynamic-update-slice_fusion.5 = bf16[7,2,2,64,1536]{4,3,2,1,0:T(8,128)(2,1)} fusion(bf16[1,2,2,64,1536]{4,3,2,1,0:T(8,128)(2,1)} %bitcast.1), kind=kLoop, calls=%fused_computation.27 | loop fusion | bytes 1572864
  51.5 0.0 collective-permute-done.1
  51.5 2.1 %constant_dynamic-update-slice_fusion.4 = bf16[7,2,2,64,1536]{4,3,2,1,0:T(8,128)(2,1)} fusion(bf16[7,2,2,64,1536]{4,3,2,1,0:T(8,128)(2,1)} %constant_dynamic-update-slice_fusion.5, bf16[1,2,2,64,1536]{4,3,2,1,0:T(8,128)(2,1)} %bitcast.3), kind=kLoop, calls=%fused_computation.26 | loop fusion | bytes 1572864
  53.6 0.5 collective-permute-done.2
  54.1 2.1 %constant_dynamic-update-slice_fusion.3 = bf16[7,2,2,64,1536]{4,3,2,1,0:T(8,128)(2,1)} fusion(bf16[7,2,2,64,1536]{4,3,2,1,0:T(8,128)(2,1)} %constant_dynamic-update-slice_fusion.4, bf16[1,2,2,64,1536]{4,3,2,1,0:T(8,128)(2,1)} %bitcast.5), kind=kLoop, calls=%fused_computation.25 | loop fusion | bytes 1572864
  56.1 0.0 copy-done.1
  56.2 0.9 fusion.18
  57.1 0.0 collective-permute-done.3
  57.1 2.1 %constant_dynamic-update-slice_fusion.2 = bf16[7,2,2,64,1536]{4,3,2,1,0:T(8,128)(2,1)} fusion(bf16[7,2,2,64,1536]{4,3,2,1,0:T(8,128)(2,1)} %fusion.18, bf16[1,2,2,64,1536]{4,3,2,1,0:T(8,128)(2,1)} %bitcast.10), kind=kLoop, calls=%fused_computation.24 | loop fusion | bytes 1572864
  59.2 0.0 collective-permute-done.4
  59.2 2.1 %constant_dynamic-update-slice_fusion.1 = bf16[7,2,2,64,1536]{4,3,2,1,0:T(8,128)(2,1)} fusion(bf16[7,2,2,64,1536]{4,3,2,1,0:T(8,128)(2,1)} %constant_dynamic-update-slice_fusion.2, bf16[1,2,2,64,1536]{4,3,2,1,0:T(8,128)(2,1)} %bitcast.12), kind=kLoop, calls=%fused_computation.23 | loop fusion | bytes 1572864
  61.2 23.5 %collective-permute-done.5 = bf16[2,1,128,1536]{3,2,0,1:T(8,128)(2,1)S(1)} collective-permute-done((bf16[2,1,128,1536]{3,2,0,1:T(8,128)(2,1)}, bf16[2,1,128,1536]{3,2,0,1:T(8,128)(2,1)S(1)}, u32[]{:S(2)}, u32[]{:S(2)}) %collective-permute-start.5) | collective-permute-done | bytes 786464 | tf_op jit(solution)/shard_map/ppermute | solution.py:17
  84.7 1.0 constant_dynamic-update-slice_fusion
  85.7 5.7 %gather_fusion = bf16[12,2,64,1536]{3,2,1,0:T(8,128)(2,1)} fusion(bf16[7,2,2,64,1536]{4,3,2,1,0:T(8,128)(2,1)} %constant_dynamic-update-slice_fusion, s32[12]{0:T(128)S(1)} %reshape.29), kind=kCustom, calls=%fused_computation | custom fusion | bytes 9437280 | tf_op jit(solution)/shard_map/gather | solution.py:36
  91.4 5.0 %fusion.26 = (bf16[2,6,1,64,1536]{4,3,2,1,0:T(8,128)(2,1)}, bf16[2,6,1,64,1536]{4,3,2,1,0:T(8,128)(2,1)}) fusion(bf16[2,6,2,64,1536]{4,3,2,1,0:T(8,128)(2,1)} %bitcast.49), kind=kLoop, calls=%fused_computation.39 | loop fusion | bytes 9437184 | tf_op jit(solution)/shard_map/slice | solution.py:37
  96.4 4.2 %reshape_squeeze.10 = bf16[2,384,12,128]{3,2,1,0:T(8,128)(2,1)S(1)} reshape(bf16[2,6,1,64,1536]{4,3,2,1,0:T(8,128)(2,1)} %get-tuple-element.5) | data formatting | bytes 4718592 | tf_op jit(solution)/shard_map/reshape;squeeze | solution.py:37
  100.5 2.2 %fusion.5 = f32[2,12,384,64]{2,3,1,0:T(8,128)S(1)} fusion(bf16[2,384,12,128]{3,2,1,0:T(8,128)(2,1)S(1)} %reshape_squeeze.10, bf16[2,64,12,128]{3,2,1,0:T(8,128)(2,1)} %reshape_squeeze.11), kind=kOutput, calls=%fused_computation.9 | convolution fusion | flops 150994944 | bytes 5111808 | tf_op jit(solution)/shard_map/bqhd,bkhd->bhqk/dot_general | solution.py:40
  102.8 0.0 copy-start
  102.8 2.0 %fusion.27 = (f32[2,12,64]{2,1,0:T(8,128)S(1)}, f32[2,12,64,384]{3,2,1,0:T(8,128)}) fusion(f32[2,12,384,64]{2,3,1,0:T(8,128)S(1)} %fusion.5), kind=kOutput, calls=%fused_computation.40 | output fusion | flops 2359679 | bytes 4724736 | tf_op jit(solution)/shard_map/sub | solution.py:44
  104.8 0.0 copy-done
  104.8 3.0 %reshape_squeeze.9 = bf16[2,384,12,128]{3,2,1,0:T(8,128)(2,1)} reshape(bf16[2,6,1,64,1536]{4,3,2,1,0:T(8,128)(2,1)S(1)} %copy-done) | data formatting | bytes 4718592 | tf_op jit(solution)/shard_map/reshape;squeeze | solution.py:38
  107.8 3.7 %fusion.13 = bf16[2,64,12,128]{3,1,2,0:T(8,128)(2,1)S(1)} fusion(bf16[2,384,12,128]{3,2,1,0:T(8,128)(2,1)} %reshape_squeeze.9, f32[2,12,64,384]{3,2,1,0:T(8,128)} %get-tuple-element.8, f32[2,12,64]{2,1,0:T(8,128)S(1)} %get-tuple-element.7), kind=kOutput, calls=%fused_computation.14 | convolution fusion | flops 152371200 | bytes 5117952 | tf_op jit(solution)/shard_map/bhqk,bkhd->bqhd/dot_general | solution.py:46
  111.5 0.3 copy.55
  111.8 6.0 %convolution_convert_fusion = bf16[128,3072]{1,0:T(8,128)(2,1)} fusion(bf16[1536,3072]{1,0:T(8,128)(2,1)} %param.6, bf16[16,8,12,128]{3,2,1,0:T(8,128)(2,1)S(1)} %bitcast.54), kind=kOutput, calls=%fused_computation.2 | convolution fusion | flops 1208352768 | bytes 10616832 | tf_op jit(solution)/shard_map/dot_general | solution.py:50
  117.7 0.0 reduce-scatter.2.cloned.1.call-update
  117.8 15.7 %reduce-scatter.2.cloned.1.call-done = bf16[64,3072]{1,0:T(8,128)(2,1)} async-done(((bf16[128,3072]{1,0:T(8,128)(2,1)}), bf16[64,3072]{1,0:T(8,128)(2,1)}) %reduce-scatter.2.cloned.1.call-update) | async-done | bytes 393232 | tf_op jit(solution)/shard_map/reduce_scatter | solution.py:49
  (1 shorter events, 0.0 us)
Async XLA Ops:
  6.5 41.6 %collective-permute-start = (bf16[2,1,128,1536]{3,2,0,1:T(8,128)(2,1)}, bf16[2,1,128,1536]{3,2,0,1:T(8,128)(2,1)}, u32[]{:S(2)}, u32[]{:S(2)}) collective-permute-start(bf16[2,1,128,1536]{3,2,0,1:T(8,128)(2,1)} %bitcast.56), channel_id=1, source_target_pairs={{0,5},{1,8},{4,9},{5,12},{8,13},{2,7},{3,10},{6,11},{7,14},{10,15}... | collective-permute-start | bytes 2359304 | tf_op jit(solution)/shard_map/ppermute | solution.py:17
  17.6 17.3 %copy-start.2 = (s32[2,6]{1,0:T(2,128)S(1)}, s32[2,6]{1,0:T(2,128)}, u32[]{:S(2)}) copy-start(s32[2,6]{1,0:T(2,128)} %param.7) | copy-start | bytes 148
  20.6 19.1 %all-to-all-start = ((bf16[2,2,147456]{2,1,0:T(2,128)(2,1)}), bf16[2,2,147456]{2,1,0:T(2,128)(2,1)}, u32[]{:S(2)}, u32[]{:S(2)}) async-start(bf16[2,2,147456]{2,1,0:T(2,128)(2,1)} %reshape.47), calls=%async_computation | async-start | bytes 2359296 | tf_op jit(solution)/shard_map/all_to_all | solution.py:21
  25.0 108.5 %reduce-scatter.2.cloned.1.call-start = ((), (), s32[]{:S(2)}) async-start(), calls=%async_computation.2 | async-start | bytes 1179648 | tf_op jit(solution)/shard_map/reduce_scatter | solution.py:49
  25.1 26.4 %collective-permute-start.1 = (bf16[2,1,128,1536]{3,2,0,1:T(8,128)(2,1)}, bf16[2,1,128,1536]{3,2,0,1:T(8,128)(2,1)}, u32[]{:S(2)}, u32[]{:S(2)}) collective-permute-start(bf16[2,1,128,1536]{3,2,0,1:T(8,128)(2,1)} %bitcast.57), channel_id=1, source_target_pairs={{0,4},{1,5},{4,8},{5,9},{8,12},{9,13},{2,6},{3,7},{6,10},{7,11},{1... | collective-permute-start | bytes 2359304 | tf_op jit(solution)/shard_map/ppermute | solution.py:17
  28.3 25.8 %collective-permute-start.2 = (bf16[2,1,128,1536]{3,2,0,1:T(8,128)(2,1)}, bf16[2,1,128,1536]{3,2,0,1:T(8,128)(2,1)}, u32[]{:S(2)}, u32[]{:S(2)}) collective-permute-start(bf16[2,1,128,1536]{3,2,0,1:T(8,128)(2,1)} %bitcast.58), channel_id=1, source_target_pairs={{0,1},{1,4},{4,5},{5,8},{8,9},{9,12},{12,13},{2,3},{3,6},{6,7},{7,... | collective-permute-start | bytes 2359304 | tf_op jit(solution)/shard_map/ppermute | solution.py:17
  30.2 26.9 %collective-permute-start.3 = (bf16[2,1,128,1536]{3,2,0,1:T(8,128)(2,1)}, bf16[2,1,128,1536]{3,2,0,1:T(8,128)(2,1)}, u32[]{:S(2)}, u32[]{:S(2)}) collective-permute-start(bf16[2,1,128,1536]{3,2,0,1:T(8,128)(2,1)} %bitcast.59), channel_id=1, source_target_pairs={{1,0},{4,1},{5,4},{8,5},{9,8},{12,9},{13,12},{3,2},{6,3},{7,6},{10... | collective-permute-start | bytes 2359304 | tf_op jit(solution)/shard_map/ppermute | solution.py:17
  33.6 25.6 %collective-permute-start.4 = (bf16[2,1,128,1536]{3,2,0,1:T(8,128)(2,1)}, bf16[2,1,128,1536]{3,2,0,1:T(8,128)(2,1)}, u32[]{:S(2)}, u32[]{:S(2)}) collective-permute-start(bf16[2,1,128,1536]{3,2,0,1:T(8,128)(2,1)} %bitcast.60), channel_id=1, source_target_pairs={{4,0},{5,1},{8,4},{9,5},{12,8},{13,9},{6,2},{7,3},{10,6},{11,7},{1... | collective-permute-start | bytes 2359304 | tf_op jit(solution)/shard_map/ppermute | solution.py:17
  45.9 10.2 %copy-start.1 = (bf16[3,1,64,2,1536]{4,2,3,0,1:T(8,128)(2,1)S(1)}, bf16[3,1,64,2,1536]{4,2,3,0,1:T(8,128)(2,1)}, u32[]{:S(2)}) copy-start(bf16[3,1,64,2,1536]{4,2,3,0,1:T(8,128)(2,1)} %copy.48) | copy-start | bytes 3538948
  48.1 36.6 %collective-permute-start.5 = (bf16[2,1,128,1536]{3,2,0,1:T(8,128)(2,1)}, bf16[2,1,128,1536]{3,2,0,1:T(8,128)(2,1)S(1)}, u32[]{:S(2)}, u32[]{:S(2)}) collective-permute-start(bf16[2,1,128,1536]{3,2,0,1:T(8,128)(2,1)} %bitcast.61), channel_id=1, source_target_pairs={{5,0},{8,1},{9,4},{12,5},{13,8},{7,2},{10,3},{11,6},{14,7},{15,10}... | collective-permute-start | bytes 2359304 | tf_op jit(solution)/shard_map/ppermute | solution.py:17
  102.8 2.0 %copy-start = (bf16[2,6,1,64,1536]{4,3,2,1,0:T(8,128)(2,1)S(1)}, bf16[2,6,1,64,1536]{4,3,2,1,0:T(8,128)(2,1)}, u32[]{:S(2)}) copy-start(bf16[2,6,1,64,1536]{4,3,2,1,0:T(8,128)(2,1)} %get-tuple-element.6) | copy-start | bytes 7077892
Sparse Core Ops, SparseCore 0:
  117.9 15.5 reduce-scatter.1
where the time goes:
time: 142 us; the launch traced here: 140 us
  local copies, waits for them, and re-layouts  46.5 us (33%)
  waiting for transfers between devices  44.4 us (31%)
  starting transfers between devices  22 us (15%)
  between operations  13.5 us (10%)
  matrix products  11.9 us (8%)
  other arithmetic  2.01 us (1%)
    ppermute x6, waiting for transfers between devices, passed_along(): return lax.ppermute(array, axis, pairs)  24 us
    unnamed x15, local copies, waits for them, and re-layouts  21.9 us
    ppermute x6, starting transfers between devices, passed_along(): return lax.ppermute(array, axis, pairs)  17.5 us
    reduce_scatter x1, waiting for transfers between devices, per_device(): lax.psum_scatter(jnp.dot(attended, w_out, preferred_element_type=jnp.floa...  15.7 us
    dot_general x1, matrix products, per_device(): jnp.dot(attended, w_out, preferred_element_type=jnp.float32)  5.96 us
    gather x1, local copies, waits for them, and re-layouts, per_device(): picked = bank[row_offset, :, column]  5.69 us
    slice x1, local copies, waits for them, and re-layouts, per_device(): keys = picked[:, :, 0].reshape(blocks, NB * BLOCK, local_heads, HD)  4.96 us
    all_to_all x1, waiting for transfers between devices, per_device(): lax.all_to_all(qkv, 'head', split_axis=3, concat_axis=2, tiled=True)  4.68 us
  transfers between devices with their start and end apart: 8, of which 4 were waited for; matrix products, arithmetic and copies ran while one was open for 20% of the time, Pallas kernels for 0%

commit v1 on v0

v1 whole, which is shorter than its diff:
```python
import functools
import math

import jax
import jax.numpy as jnp
from jax import lax
from jax.experimental import pallas as pl
from jax.experimental.pallas import tpu as pltpu
from jax.sharding import PartitionSpec as P

HD = 128
BLOCK = 64
NB = 6
REACH = 3
MESH = pl.DeviceIdType.MESH


def head_cuts(local_heads):
    if local_heads % 4 == 0:
        return [4] * (local_heads // 4)
    return [1] * local_heads


def column_piece(total):
    for size in (768, 512, 256, 128):
        if total % size == 0:
            return size
    return total


def kernel(
    heads, chips, cuts, piece,
    near_ref, qkv_ref, stale_ref, w_ref, out_ref,
    w_buf, acc, att, sent, landed, banks, asked,
    w_sem, fill_send, fill_recv, own_send, bank_recv, bank_send, part_send, part_recv,
):
    z = lax.axis_index("patch")
    h = lax.axis_index("head")
    s = lax.axis_index("sub")
    row = 2 * z + s
    blocks = stale_ref.shape[1]
    rows = qkv_ref.shape[2]
    width = stale_ref.shape[3]
    depth = out_ref.shape[2]
    has_left = z > 0
    has_right = z < chips - 1
    core0 = s == 0
    has_diag = jnp.logical_or(jnp.logical_and(core0, has_left), jnp.logical_and(s == 1, has_right))
    diag_z = jnp.where(core0, jnp.maximum(z - 1, 0), jnp.minimum(z + 1, chips - 1))
    left = {"patch": jnp.maximum(z - 1, 0)}
    right = {"patch": jnp.minimum(z + 1, chips - 1)}
    sibling = {"sub": 1 - s}
    diag = {"patch": diag_z, "sub": 1 - s}
    peers = [lax.rem(h + k, heads) for k in range(1, heads)]
    sources = [lax.rem(h - k + heads, heads) for k in range(1, heads)]

    barrier = pltpu.get_barrier_semaphore()

    @pl.when(has_left)
    def _():
        pl.semaphore_signal(barrier, inc=1, device_id=left, device_id_type=MESH)

    @pl.when(has_right)
    def _():
        pl.semaphore_signal(barrier, inc=1, device_id=right, device_id_type=MESH)

    @pl.when(has_diag)
    def _():
        pl.semaphore_signal(barrier, inc=1, device_id=diag, device_id_type=MESH)

    pl.semaphore_signal(barrier, inc=1, device_id=sibling, device_id_type=MESH)
    for peer in peers:
        pl.semaphore_signal(barrier, inc=1, device_id={"head": peer}, device_id_type=MESH)

    starts = [sum(cuts[:c]) * HD for c in range(len(cuts))]

    def row_at(c, slot):
        return banks[c].at[:, pl.ds(slot * blocks, blocks)]

    def remote(src, dst, send, recv, device):
        return pltpu.make_async_remote_copy(
            src_ref=src, dst_ref=dst, send_sem=send, recv_sem=recv,
            device_id=device, device_id_type=MESH,
        )

    def fresh_dst(c, owner):
        first = owner * rows
        block = REACH * blocks + first // BLOCK
        inside = pl.multiple_of(first % BLOCK, rows)
        return (
            asked[c].at[pl.ds(pl.multiple_of(first, rows), rows)],
            banks[c].at[:, block, pl.ds(inside, rows)],
        )

    def fresh_src(c, owner):
        cols = pl.ds(pl.multiple_of(owner * width + starts[c], HD), cuts[c] * HD)
        return qkv_ref.at[0, 0, :, cols], qkv_ref.at[1:3, 0, :, cols]

    def local_fill(c):
        src, dst = fresh_src(c, h), fresh_dst(c, h)
        return [pltpu.make_async_copy(src[i], dst[i], w_sem.at[1 + i, c]) for i in range(2)]

    def w_fill(c):
        part = pl.ds(starts[c], cuts[c] * HD)
        return pltpu.make_async_copy(w_ref.at[part], w_buf.at[part], w_sem.at[0, c])

    def fresh_to(c, k):
        src, dst = fresh_src(c, peers[k]), fresh_dst(c, h)
        return [
            remote(src[i], dst[i], fill_send.at[c, k, i], fill_recv.at[c, k, i], {"head": peers[k]})
            for i in range(2)
        ]

    def fresh_from(c, k):
        src, dst = fresh_src(c, h), fresh_dst(c, sources[k])
        return [
            remote(src[i], dst[i], fill_send.at[c, k, i], fill_recv.at[c, k, i], {"head": peers[k]})
            for i in range(2)
        ]

    def own(c):
        return stale_ref.at[:, :, :, starts[c]:starts[c] + cuts[c] * HD]

    def to_right(c):
        return remote(own(c), row_at(c, 1), own_send.at[c, 0], bank_recv.at[c, 0], right)

    def to_left(c):
        return remote(own(c), row_at(c, 5), own_send.at[c, 1], bank_recv.at[c, 1], left)

    sib_own = jnp.where(core0, 2, 4)
    sib_left = jnp.where(core0, 0, 2)
    sib_right = jnp.where(core0, 4, 6)
    my_own = jnp.where(core0, 4, 2)
    my_left = jnp.where(core0, 2, 0)
    my_right = jnp.where(core0, 6, 4)

    def own_sib(c, slot):
        return remote(own(c), row_at(c, slot), own_send.at[c, 2], bank_recv.at[c, 2], sibling)

    def left_sib(c, slot):
        return remote(row_at(c, 1), row_at(c, slot), bank_send.at[c, 0], bank_recv.at[c, 3], sibling)

    def right_sib(c, slot):
        return remote(row_at(c, 5), row_at(c, slot), bank_send.at[c, 1], bank_recv.at[c, 4], sibling)

    def far(c, src, dst):
        return remote(row_at(c, src), row_at(c, dst), bank_send.at[c, 2], bank_recv.at[c, 5], diag)

    inner = jnp.logical_and(has_left, has_right)
    far_src = jnp.where(core0, 5, 1)
    far_dst = jnp.where(core0, 6, 0)
    far_mine = jnp.where(core0, 0, 6)
    has_far = jnp.logical_or(jnp.logical_and(core0, z >= 2), jnp.logical_and(s == 1, z <= chips - 3))

    for c in range(len(cuts)):
        for copy in local_fill(c):
            copy.start()
        w_fill(c).start()

    count = (
        heads + has_left.astype(jnp.int32) + has_right.astype(jnp.int32) + has_diag.astype(jnp.int32)
    )
    pl.semaphore_wait(barrier, count)

    for c in range(len(cuts)):
        @pl.when(has_right)
        def _():
            to_right(c).start()

        @pl.when(has_left)
        def _():
            to_left(c).start()

        for k in range(heads - 1):
            for copy in fresh_to(c, k):
                copy.start()
        own_sib(c, sib_own).start()

    def pass_on(c):
        @pl.when(has_left)
        def _():
            to_left_arrived = remote(own(c), row_at(c, 1), own_send.at[c, 0], bank_recv.at[c, 0], right)
            to_left_arrived.wait_recv()

        @pl.when(has_right)
        def _():
            remote(own(c), row_at(c, 5), own_send.at[c, 1], bank_recv.at[c, 1], left).wait_recv()

        @pl.when(inner)
        def _():
            far(c, far_src, far_dst).start()

        @pl.when(has_left)
        def _():
            left_sib(c, sib_left).start()

        @pl.when(has_right)
        def _():
            right_sib(c, sib_right).start()

    def arrived(c):
        for copy in local_fill(c):
            copy.wait()
        for k in range(heads - 1):
            for copy in fresh_from(c, k):
                copy.wait_recv()
        own_sib(c, my_own).wait_recv()

        @pl.when(has_left)
        def _():
            left_sib(c, my_left).wait_recv()

        @pl.when(has_right)
        def _():
            right_sib(c, my_right).wait_recv()

        @pl.when(has_far)
        def _():
            far(c, far_src, far_mine).wait_recv()

    first_block = (row - REACH) * blocks
    scale = 1.0 / math.sqrt(HD)

    def attend(c):
        for b in range(blocks):
            listed = [
                jnp.clip(near_ref[b, n] - first_block, 0, banks[c].shape[1] - 1) for n in range(NB)
            ]
            for head in range(cuts[c]):
                cols = slice(head * HD, (head + 1) * HD)
                query = asked[c][b * BLOCK:(b + 1) * BLOCK, cols]
                keys = jnp.concatenate([banks[c][0, n, :, cols] for n in listed], axis=0)
                values = jnp.concatenate([banks[c][1, n, :, cols] for n in listed], axis=0)
                scores = lax.dot_general(
                    query, keys, (((1,), (1,)), ((), ())), preferred_element_type=jnp.float32
                ) * scale
                top = jnp.max(scores, axis=-1, keepdims=True)
                expo = jnp.exp(scores - top)
                weights = (expo * (1.0 / jnp.sum(expo, axis=-1, keepdims=True))).astype(jnp.bfloat16)
                got = jnp.dot(weights, values, preferred_element_type=jnp.float32)
                att[b * BLOCK:(b + 1) * BLOCK, starts[c] + head * HD:starts[c] + (head + 1) * HD] = (
                    got.astype(jnp.bfloat16)
                )

    def product(c, columns):
        part = slice(starts[c], starts[c] + cuts[c] * HD)
        return jnp.dot(att[:, part], w_buf[part, columns], preferred_element_type=jnp.float32)

    def project(c):
        w_fill(c).wait()

        @pl.loop(0, depth // piece)
        def _(j):
            columns = pl.ds(pl.multiple_of(j * piece, piece), piece)
            if c == 0:
                acc[:, columns] = product(c, columns)
            else:
                acc[:, columns] += product(c, columns)

    last = len(cuts) - 1
    pass_on(0)
    for c in range(last):
        pass_on(c + 1)
        arrived(c)
        attend(c)
        project(c)
    arrived(last)
    attend(last)
    w_fill(last).wait()

    def part_to(j, k):
        columns = slice(j * piece, (j + 1) * piece)
        mine = pl.ds(pl.multiple_of(peers[k] * rows, rows), rows)
        return remote(
            sent.at[mine, columns], landed.at[k, :, columns],
            part_send.at[k, j], part_recv.at[k, j], {"head": peers[k]},
        )

    for j in range(depth // piece):
        columns = slice(j * piece, (j + 1) * piece)
        total = product(last, columns)
        if last > 0:
            total = total + acc[:, columns]
        sent[:, columns] = total.astype(jnp.bfloat16)
        for k in range(heads - 1):
            part_to(j, k).start()

    own_rows = pl.ds(pl.multiple_of(h * rows, rows), rows)
    for j in range(depth // piece):
        columns = slice(j * piece, (j + 1) * piece)
        total = sent[own_rows, columns].astype(jnp.float32)
        for k in range(heads - 1):
            part_to(j, k).wait_recv()
            total = total + landed[k, :, columns].astype(jnp.float32)
        out_ref[0, :, columns] = total.astype(jnp.bfloat16)

    for c in range(len(cuts)):
        @pl.when(has_right)
        def _():
            to_right(c).wait_send()
            right_sib(c, sib_right).wait_send()

        @pl.when(has_left)
        def _():
            to_left(c).wait_send()
            left_sib(c, sib_left).wait_send()

        @pl.when(inner)
        def _():
            far(c, far_src, far_dst).wait_send()

        own_sib(c, sib_own).wait_send()
        for k in range(heads - 1):
            for copy in fresh_to(c, k):
                copy.wait_send()
    for j in range(depth // piece):
        for k in range(heads - 1):
            part_to(j, k).wait_send()


def per_device(heads, chips, qkv, stale_kv, w_out, neighbors):
    rows = qkv.shape[2]
    tokens = stale_kv.shape[2]
    width, depth = w_out.shape
    blocks = tokens // BLOCK
    cuts = head_cuts(width // HD)
    piece = column_piece(depth)
    pieces = depth // piece
    others = heads - 1
    count = len(cuts)
    bf16 = jnp.bfloat16
    stale = stale_kv.reshape(2, blocks, BLOCK, width)
    slots = (2 * REACH + 1) * blocks
    dma = pltpu.SemaphoreType.DMA
    return pl.pallas_call(
        functools.partial(kernel, heads, chips, cuts, piece),
        out_shape=jax.ShapeDtypeStruct((1, rows, depth), bf16),
        in_specs=[
            pl.BlockSpec(memory_space=pltpu.SMEM),
            pl.BlockSpec(memory_space=pl.ANY),
            pl.BlockSpec(memory_space=pl.ANY),
            pl.BlockSpec(memory_space=pl.ANY),
        ],
        out_specs=pl.BlockSpec(memory_space=pltpu.VMEM),
        scratch_shapes=[
            pltpu.VMEM((width, depth), bf16),
            pltpu.VMEM((tokens, depth), jnp.float32),
            pltpu.VMEM((tokens, width), bf16),
            pltpu.VMEM((tokens, depth), bf16),
            pltpu.VMEM((others, rows, depth), bf16),
            [pltpu.VMEM((2, slots, BLOCK, cut * HD), bf16) for cut in cuts],
            [pltpu.VMEM((tokens, cut * HD), bf16) for cut in cuts],
            dma((3, count)),
            dma((count, others, 2)),
            dma((count, others, 2)),
            dma((count, 3)),
            dma((count, 6)),
            dma((count, 3)),
            dma((others, pieces)),
            dma((others, pieces)),
        ],
        compiler_params=pltpu.CompilerParams(
            collective_id=0, has_side_effects=True, vmem_limit_bytes=48 * 2 ** 20
        ),
        name="windowed",
    )(neighbors, qkv, stale, w_out)


def solution(mesh):
    placed = (
        P(None, ("group", "patch", "sub"), "head", None),
        P(None, ("group", "patch", "sub"), None, "head"),
        P("head", None),
        P(("group", "patch", "sub"), None),
    )
    sizes = dict(mesh.shape)
    return jax.shard_map(
        functools.partial(per_device, sizes["head"], sizes["patch"]),
        mesh=mesh,
        in_specs=placed,
        out_specs=P(("group", "patch", "sub"), "head", None),
        check_vma=False,
    )
```

time: 142 us -> 49.3 us (0.35)
  Pallas kernels: 0 us -> 45.2 us
  waiting for transfers between devices: 44.4 us -> 0 us
  local copies, waits for them, and re-layouts: 46.5 us -> 3.83 us
  starting transfers between devices: 22 us -> 0 us
  between operations: 13.5 us -> 0.01 us
  matrix products: 11.9 us -> 0 us
  other arithmetic: 2.01 us -> 0 us
    pallas_call x0 -> x1, Pallas kernels: none -> 45.2 us  [per_device(): pl.pallas_call(functools.partial(kernel, heads, chips, cuts, piece), out_...]
    ppermute x6 -> x0, waiting for transfers between devices: 24 us -> none  [passed_along(): return lax.ppermute(array, axis, pairs)]
    unnamed x15 -> x7, local copies, waits for them, and re-layouts: 21.9 us -> 3.83 us
    ppermute x6 -> x0, starting transfers between devices: 17.5 us -> none  [passed_along(): return lax.ppermute(array, axis, pairs)]
    reduce_scatter x1 -> x0, waiting for transfers between devices: 15.7 us -> none  [per_device(): lax.psum_scatter(jnp.dot(attended, w_out, preferred_element_type=jnp.floa...]
    dot_general x3 -> x0, matrix products: 11.9 us -> none  [the longest x1 5.96 us: per_device(): jnp.dot(attended, w_out, preferred_element_type=jnp.float32)]
    another operation x4 -> x0, local copies, waits for them, and re-layouts: 9.24 us -> none  [the longest x1 4.16 us: per_device(): keys = picked[:, :, 0].reshape(blocks, NB * BLOCK, local_heads, HD)]
    slice x2 -> x0, local copies, waits for them, and re-layouts: 6.08 us -> none  [the longest x1 4.96 us: per_device(): keys = picked[:, :, 0].reshape(blocks, NB * BLOCK, local_heads, HD)]
  transfers between devices with their start and end apart: 8 -> 0, of which waited for: 4 -> 0; matrix products, arithmetic and copies ran while one was open for 20% -> 0% of each run, Pallas kernels for 0% -> 0%
where the time goes in v1:
time: 49.3 us; the launch traced here: 49.1 us
  Pallas kernels  45.2 us (92%)
  local copies, waits for them, and re-layouts  3.83 us (8%)
    pallas_call x1, Pallas kernels, per_device(): pl.pallas_call(functools.partial(kernel, heads, chips, cuts, piece), out_...  45.2 us
    unnamed x7, local copies, waits for them, and re-layouts  3.83 us

profile of v1, /device:TPU:1, one launch (start us, length us, event | category | flops | bytes accessed | tf_op | source)
XLA Modules:
  0.0 49.1 jit_solution(9208679185403138354)
XLA Ops:
  0.0 0.0 copy-start
  0.0 1.3 %copy-done = bf16[3,1,64,3072]{3,2,1,0:T(8,128)(2,1)S(1)} copy-done((bf16[3,1,64,3072]{3,2,1,0:T(8,128)(2,1)S(1)}, bf16[3,1,64,3072]{3,2,1,0:T(8,128)(2,1)}, u32[]{:S(2)}) %copy-start) | copy-done | bytes 1179672
  1.3 0.0 copy-start.1
  1.3 1.1 %copy-done.1 = bf16[2,1,128,1536]{3,2,1,0:T(8,128)(2,1)S(1)} copy-done((bf16[2,1,128,1536]{3,2,1,0:T(8,128)(2,1)S(1)}, bf16[2,1,128,1536]{3,2,1,0:T(8,128)(2,1)}, u32[]{:S(2)}) %copy-start.1) | copy-done | bytes 786456
  2.4 0.0 copy-start.2
  2.4 0.7 %copy-done.2 = s32[2,6]{1,0:T(2,128)S(1)} copy-done((s32[2,6]{1,0:T(2,128)S(1)}, s32[2,6]{1,0:T(2,128)}, u32[]{:S(2)}) %copy-start.2) | copy-done | bytes 72
  3.1 45.2 %windowed.1 = bf16[1,64,3072]{2,1,0:T(8,128)(2,1)S(1)} custom-call(s32[2,6]{1,0:T(2,128)S(1)} %copy-done.2, bf16[3,1,64,3072]{3,2,1,0:T(8,128)(2,1)S(1)} %copy-done, bf16[2,2,64,1536]{3,2,1,0:T(8,128)(2,1)S(1)} %bitcast.1, bf16[1536,3072]{1,0:T(8,128)(2,1)} %w_ref.1), custom_call_target="tpu_custom_call" | custom-call | tf_op jit(solution)/shard_map/windowed/pallas_call | solution.py:335
  48.3 0.7 %copy.6 = bf16[1,64,3072]{2,1,0:T(8,128)(2,1)} copy(bf16[1,64,3072]{2,1,0:T(8,128)(2,1)S(1)} %windowed.1) | data formatting | bytes 786432
Async XLA Ops:
  0.0 1.3 %copy-start = (bf16[3,1,64,3072]{3,2,1,0:T(8,128)(2,1)S(1)}, bf16[3,1,64,3072]{3,2,1,0:T(8,128)(2,1)}, u32[]{:S(2)}) copy-start(bf16[3,1,64,3072]{3,2,1,0:T(8,128)(2,1)} %qkv_ref.1) | copy-start | bytes 3538948
  1.3 1.1 %copy-start.1 = (bf16[2,1,128,1536]{3,2,1,0:T(8,128)(2,1)S(1)}, bf16[2,1,128,1536]{3,2,1,0:T(8,128)(2,1)}, u32[]{:S(2)}) copy-start(bf16[2,1,128,1536]{3,2,1,0:T(8,128)(2,1)} %param.5) | copy-start | bytes 2359300
  2.4 0.7 %copy-start.2 = (s32[2,6]{1,0:T(2,128)S(1)}, s32[2,6]{1,0:T(2,128)}, u32[]{:S(2)}) copy-start(s32[2,6]{1,0:T(2,128)} %near_ref.1) | copy-start | bytes 148

commit v2 on v1

--- a/solution.py
+++ b/solution.py
@@ -16,8 +16,8 @@
 
 
 def head_cuts(local_heads):
-    if local_heads % 4 == 0:
-        return [4] * (local_heads // 4)
+    if local_heads % 6 == 0:
+        return [6] * (local_heads // 6)
     return [1] * local_heads
 
 
@@ -219,32 +219,40 @@
             far(c, far_src, far_mine).wait_recv()
 
     first_block = (row - REACH) * blocks
-    scale = 1.0 / math.sqrt(HD)
-
-    def attend(c):
-        for b in range(blocks):
-            listed = [
-                jnp.clip(near_ref[b, n] - first_block, 0, banks[c].shape[1] - 1) for n in range(NB)
-            ]
-            for head in range(cuts[c]):
-                cols = slice(head * HD, (head + 1) * HD)
-                query = asked[c][b * BLOCK:(b + 1) * BLOCK, cols]
-                keys = jnp.concatenate([banks[c][0, n, :, cols] for n in listed], axis=0)
-                values = jnp.concatenate([banks[c][1, n, :, cols] for n in listed], axis=0)
-                scores = lax.dot_general(
-                    query, keys, (((1,), (1,)), ((), ())), preferred_element_type=jnp.float32
-                ) * scale
-                top = jnp.max(scores, axis=-1, keepdims=True)
-                expo = jnp.exp(scores - top)
-                weights = (expo * (1.0 / jnp.sum(expo, axis=-1, keepdims=True))).astype(jnp.bfloat16)
-                got = jnp.dot(weights, values, preferred_element_type=jnp.float32)
-                att[b * BLOCK:(b + 1) * BLOCK, starts[c] + head * HD:starts[c] + (head + 1) * HD] = (
-                    got.astype(jnp.bfloat16)
-                )
-
-    def product(c, columns):
+    scale = math.log2(math.e) / math.sqrt(HD)
+
+    def attend(c, b):
+        tokens = pl.ds(pl.multiple_of(b * BLOCK, BLOCK), BLOCK)
+        most = banks[c].shape[1] - 1
+        listed = [jnp.clip(near_ref[b, n] - first_block, 0, most) for n in range(NB)]
+        spans = [slice(head * HD, (head + 1) * HD) for head in range(cuts[c])]
+        scores = [
+            lax.dot_general(
+                asked[c][tokens, cols],
+                jnp.concatenate([banks[c][0, n, :, cols] for n in listed], axis=0),
+                (((1,), (1,)), ((), ())),
+                preferred_element_type=jnp.float32,
+            )
+            for cols in spans
+        ]
+        tops = [jnp.max(score, axis=-1, keepdims=True) for score in scores]
+        expos = [jnp.exp2((score - top) * scale) for score, top in zip(scores, tops)]
+        got = [
+            jnp.dot(
+                expo.astype(jnp.bfloat16),
+                jnp.concatenate([banks[c][1, n, :, cols] for n in listed], axis=0),
+                preferred_element_type=jnp.float32,
+            )
+            for expo, cols in zip(expos, spans)
+        ]
+        sums = [jnp.sum(expo, axis=-1, keepdims=True) for expo in expos]
+        for head in range(cuts[c]):
+            first = starts[c] + head * HD
+            att[tokens, first:first + HD] = (got[head] * (1.0 / sums[head])).astype(jnp.bfloat16)
+
+    def product(c, tokens, columns):
         part = slice(starts[c], starts[c] + cuts[c] * HD)
-        return jnp.dot(att[:, part], w_buf[part, columns], preferred_element_type=jnp.float32)
+        return jnp.dot(att[tokens, part], w_buf[part, columns], preferred_element_type=jnp.float32)
 
     def project(c):
         w_fill(c).wait()
@@ -253,44 +261,55 @@
         def _(j):
             columns = pl.ds(pl.multiple_of(j * piece, piece), piece)
             if c == 0:
-                acc[:, columns] = product(c, columns)
+                acc[:, columns] = product(c, slice(None), columns)
             else:
-                acc[:, columns] += product(c, columns)
+                acc[:, columns] += product(c, slice(None), columns)
 
     last = len(cuts) - 1
     pass_on(0)
     for c in range(last):
         pass_on(c + 1)
         arrived(c)
-        attend(c)
+        for b in range(blocks):
+            attend(c, b)
         project(c)
     arrived(last)
-    attend(last)
     w_fill(last).wait()
 
-    def part_to(j, k):
+    def part_to(j, k, peer):
         columns = slice(j * piece, (j + 1) * piece)
-        mine = pl.ds(pl.multiple_of(peers[k] * rows, rows), rows)
+        mine = pl.ds(pl.multiple_of(peer * rows, rows), rows)
         return remote(
             sent.at[mine, columns], landed.at[k, :, columns],
-            part_send.at[k, j], part_recv.at[k, j], {"head": peers[k]},
+            part_send.at[k, j], part_recv.at[k, j], {"head": peer},
         )
 
-    for j in range(depth // piece):
-        columns = slice(j * piece, (j + 1) * piece)
-        total = product(last, columns)
-        if last > 0:
-            total = total + acc[:, columns]
-        sent[:, columns] = total.astype(jnp.bfloat16)
-        for k in range(heads - 1):
-            part_to(j, k).start()
+    per_block = BLOCK // rows
+    for i in range(blocks):
+        b = lax.rem(h // per_block + 1 + i, blocks)
+        tokens = pl.ds(pl.multiple_of(b * BLOCK, BLOCK), BLOCK)
+        attend(last, b)
+        for j in range(depth // piece):
+            columns = slice(j * piece, (j + 1) * piece)
+            total = product(last, tokens, columns)
+            if last > 0:
+                total = total + acc[tokens, columns]
+            sent[tokens, columns] = total.astype(jnp.bfloat16)
+            for q in range(per_block):
+                peer = b * per_block + q
+                if per_block > 1:
+                    @pl.when(peer != h)
+                    def _():
+                        part_to(j, lax.rem(peer - h + heads - 1, heads), peer).start()
+                elif i < blocks - 1:
+                    part_to(j, lax.rem(peer - h + heads - 1, heads), peer).start()
 
     own_rows = pl.ds(pl.multiple_of(h * rows, rows), rows)
     for j in range(depth // piece):
         columns = slice(j * piece, (j + 1) * piece)
         total = sent[own_rows, columns].astype(jnp.float32)
         for k in range(heads - 1):
-            part_to(j, k).wait_recv()
+            part_to(j, k, peers[k]).wait_recv()
             total = total + landed[k, :, columns].astype(jnp.float32)
         out_ref[0, :, columns] = total.astype(jnp.bfloat16)
 
@@ -315,7 +334,7 @@
                 copy.wait_send()
     for j in range(depth // piece):
         for k in range(heads - 1):
-            part_to(j, k).wait_send()
+            part_to(j, k, peers[k]).wait_send()
 
 
 def per_device(heads, chips, qkv, stale_kv, w_out, neighbors):
@@ -360,7 +379,7 @@
             dma((others, pieces)),
         ],
         compiler_params=pltpu.CompilerParams(
-            collective_id=0, has_side_effects=True, vmem_limit_bytes=48 * 2 ** 20
+            collective_id=0, has_side_effects=True, vmem_limit_bytes=62 * 2 ** 20
         ),
         name="windowed",
     )(neighbors, qkv, stale, w_out)

time: 49.3 us -> 41.9 us (0.85)
  Pallas kernels: 45.2 us -> 40 us
  local copies, waits for them, and re-layouts: 3.83 us -> 1.77 us
    pallas_call x1, Pallas kernels: 45.2 us -> 40 us  [per_device(): pl.pallas_call(functools.partial(kernel, heads, chips, cuts, piece), out_...]
    unnamed x7 -> x1, local copies, waits for them, and re-layouts: 3.83 us -> 1.77 us
where the time goes in v2:
time: 41.9 us; the launch traced here: 41.8 us
  Pallas kernels  40 us (95%)
  local copies, waits for them, and re-layouts  1.77 us (4%)
    pallas_call x1, Pallas kernels, per_device(): pl.pallas_call(functools.partial(kernel, heads, chips, cuts, piece), out_...  40 us
    unnamed x1, local copies, waits for them, and re-layouts  1.77 us

profile of v2, /device:TPU:1, one launch (start us, length us, event | category | flops | bytes accessed | tf_op | source)
XLA Modules:
  0.0 41.8 jit_solution(2962791835214795550)
XLA Ops:
  0.0 40.0 %windowed.1 = bf16[1,64,3072]{2,1,0:T(8,128)(2,1)} custom-call(s32[2,6]{1,0:T(2,128)} %near_ref.1, bf16[3,1,64,3072]{3,2,1,0:T(8,128)(2,1)} %qkv_ref.1, bf16[2,2,64,1536]{3,2,1,0:T(8,128)(2,1)} %bitcast.1, bf16[1536,3072]{1,0:T(8,128)(2,1)} %w_ref.1), custom_call_target="tpu_custom_call" | custom-call | tf_op jit(solution)/shard_map/windowed/pallas_call | solution.py:354
  40.0 1.8 %copy.6 = bf16[1,64,3072]{2,1,0:T(8,128)(2,1)} copy(bf16[1,64,3072]{2,1,0:T(8,128)(2,1)} %windowed.1) | data formatting | bytes 786432

commit v3 on v2

--- a/solution.py
+++ b/solution.py
@@ -237,6 +237,8 @@
         ]
         tops = [jnp.max(score, axis=-1, keepdims=True) for score in scores]
         expos = [jnp.exp2((score - top) * scale) for score, top in zip(scores, tops)]
+        sums = [jnp.sum(expo, axis=-1, keepdims=True) for expo in expos]
+        expos = [expo * (1.0 / total) for expo, total in zip(expos, sums)]
         got = [
             jnp.dot(
                 expo.astype(jnp.bfloat16),
@@ -245,10 +247,9 @@
             )
             for expo, cols in zip(expos, spans)
         ]
-        sums = [jnp.sum(expo, axis=-1, keepdims=True) for expo in expos]
         for head in range(cuts[c]):
             first = starts[c] + head * HD
-            att[tokens, first:first + HD] = (got[head] * (1.0 / sums[head])).astype(jnp.bfloat16)
+            att[tokens, first:first + HD] = got[head].astype(jnp.bfloat16)
 
     def product(c, tokens, columns):
         part = slice(starts[c], starts[c] + cuts[c] * HD)

time: 41.9 us -> 42 us (level)
  no operation moved by 1% of the time
where the time goes in v3:
time: 42 us; the launch traced here: 41.8 us
  Pallas kernels  40 us (95%)
  local copies, waits for them, and re-layouts  1.77 us (4%)
    pallas_call x1, Pallas kernels, per_device(): pl.pallas_call(functools.partial(kernel, heads, chips, cuts, piece), out_...  40 us
    unnamed x1, local copies, waits for them, and re-layouts  1.77 us

profile of v3, /device:TPU:1, one launch (start us, length us, event | category | flops | bytes accessed | tf_op | source)
XLA Modules:
  0.0 41.8 jit_solution(5220210100783783753)
XLA Ops:
  0.0 40.0 %windowed.1 = bf16[1,64,3072]{2,1,0:T(8,128)(2,1)} custom-call(s32[2,6]{1,0:T(2,128)} %near_ref.1, bf16[3,1,64,3072]{3,2,1,0:T(8,128)(2,1)} %qkv_ref.1, bf16[2,2,64,1536]{3,2,1,0:T(8,128)(2,1)} %bitcast.1, bf16[1536,3072]{1,0:T(8,128)(2,1)} %w_ref.1), custom_call_target="tpu_custom_call" | custom-call | tf_op jit(solution)/shard_map/windowed/pallas_call | solution.py:355
  40.1 1.8 %copy.6 = bf16[1,64,3072]{2,1,0:T(8,128)(2,1)} copy(bf16[1,64,3072]{2,1,0:T(8,128)(2,1)} %windowed.1) | data formatting | bytes 786432

commit v4 on v3

--- a/solution.py
+++ b/solution.py
@@ -380,7 +380,7 @@
             dma((others, pieces)),
         ],
         compiler_params=pltpu.CompilerParams(
-            collective_id=0, has_side_effects=True, vmem_limit_bytes=62 * 2 ** 20
+            collective_id=0, has_side_effects=True, vmem_limit_bytes=53 * 2 ** 20
         ),
         name="windowed",
     )(neighbors, qkv, stale, w_out)

time: 42 us -> 40.8 us (0.971)
  Pallas kernels: 40 us -> 39.2 us
    pallas_call x1, Pallas kernels: 40 us -> 39.2 us  [per_device(): pl.pallas_call(functools.partial(kernel, heads, chips, cuts, piece), out_...]
    unnamed x1 -> x3, local copies, waits for them, and re-layouts: 1.77 us -> 1.43 us
where the time goes in v4:
time: 40.8 us; the launch traced here: 40.6 us
  Pallas kernels  39.2 us (96%)
  local copies, waits for them, and re-layouts  1.43 us (4%)
    pallas_call x1, Pallas kernels, per_device(): pl.pallas_call(functools.partial(kernel, heads, chips, cuts, piece), out_...  39.2 us
    unnamed x3, local copies, waits for them, and re-layouts  1.43 us

profile of v4, /device:TPU:1, one launch (start us, length us, event | category | flops | bytes accessed | tf_op | source)
XLA Modules:
  0.0 40.6 jit_solution(3074970478012635237)
XLA Ops:
  0.0 0.0 copy-start
  0.0 0.7 %copy-done = s32[2,6]{1,0:T(2,128)S(1)} copy-done((s32[2,6]{1,0:T(2,128)S(1)}, s32[2,6]{1,0:T(2,128)}, u32[]{:S(2)}) %copy-start) | copy-done | bytes 72
  0.7 39.2 %windowed.1 = bf16[1,64,3072]{2,1,0:T(8,128)(2,1)S(1)} custom-call(s32[2,6]{1,0:T(2,128)S(1)} %copy-done, bf16[3,1,64,3072]{3,2,1,0:T(8,128)(2,1)} %qkv_ref.1, bf16[2,2,64,1536]{3,2,1,0:T(8,128)(2,1)} %bitcast.1, bf16[1536,3072]{1,0:T(8,128)(2,1)} %w_ref.1), custom_call_target="tpu_custom_call" | custom-call | tf_op jit(solution)/shard_map/windowed/pallas_call | solution.py:355
  39.9 0.7 %copy.6 = bf16[1,64,3072]{2,1,0:T(8,128)(2,1)} copy(bf16[1,64,3072]{2,1,0:T(8,128)(2,1)S(1)} %windowed.1) | data formatting | bytes 786432
Async XLA Ops:
  0.0 0.7 %copy-start = (s32[2,6]{1,0:T(2,128)S(1)}, s32[2,6]{1,0:T(2,128)}, u32[]{:S(2)}) copy-start(s32[2,6]{1,0:T(2,128)} %near_ref.1) | copy-start | bytes 148
